TPU v7x, 32 devices: a whole 2x2x4 slice. The times are simulated.
32 devices in a mesh: gx: 16 (over z, y, core), gy: 2 (over x).
Axes of the slice: x: 2, y: 2, z: 4, core: 2. Of those that a mesh axis runs over, the one named last changes fastest.
Arguments:
- scalar: float32 [128, 256, 256], P('gx', 'gy'), may hold values from -6 to 6
- velocity: float32 [3, 128, 256, 256], P(None, 'gx', 'gy'), may hold values from -4 to 4
- weights: float32 [1024, 256], replicated, may hold values from -0.03125 to 0.03125
- ray_start: int32 [128, 1024], P('gx'), may hold values from 0 to 255
- ray_length: int32 [128, 1024], P('gx'), may hold values from 1 to 256, as said below
- pixel_of_ray: int32 [1024], replicated, may hold values from 0 to 1023, each once
- observed: float32 [128, 1024], P('gx'), may hold values from 0.3 to 3
Outputs:
- images: float32 [128, 1024], P('gx', 'gy')
- grad_scalar: float32 [128, 256, 256], P('gx', 'gy')
- grad_velocity: float32 [3, 128, 256, 256], P(None, 'gx', 'gy')
Inputs may be any that keep to these rules, and one draw needn't show every extreme that they name: Each ray covers ray_length consecutive y cells from ray_start, wrapping around periodically. `pixel_of_ray`: each pixel receives exactly one ray.
All inputs are finite; a program needn't handle non-finite values.
Results may differ from a plain program's by a relative error of at most 0.0003.
Values sent between devices are 32-bit elements; how exact they have to be, the bound alone decides.
A program may use at most 128 MiB of HBM per device.

v0:
```python
import jax
import jax.numpy as jnp
from jax import lax
from jax.sharding import PartitionSpec as P

STEPS = 3


time_step = 0.1
diffusion = 1.0


def with_halo(cells, sides, width):
    for axis, dim in sides:
        count = lax.axis_size(axis)
        head = lax.slice_in_dim(cells, 0, width, axis=dim)
        tail = lax.slice_in_dim(cells, cells.shape[dim] - width, cells.shape[dim], axis=dim)
        cells = jnp.concatenate(
            [
                lax.ppermute(tail, axis, [(i, (i + 1) % count) for i in range(count)]),
                cells,
                lax.ppermute(head, axis, [((i + 1) % count, i) for i in range(count)]),
            ],
            axis=dim,
        )
    return cells


def vertical(field):
    zeros = jnp.zeros_like(field[..., :1])
    upper = jnp.concatenate([field[..., 1:], zeros], -1)
    lower = jnp.concatenate([zeros, field[..., :-1]], -1)
    return (upper, lower)


def neighbours(padded):
    centre = padded[..., 1:-1, 1:-1, :]
    east = padded[..., 2:, 1:-1, :]
    west = padded[..., :-2, 1:-1, :]
    north = padded[..., 1:-1, 2:, :]
    south = padded[..., 1:-1, :-2, :]
    upper, lower = vertical(centre)
    return (centre, east, west, north, south, upper, lower)


def surround(field):
    return with_halo(field, (("gx", 0), ("gy", 1)), 1)


def per_device(scalar, velocity, weights, ray_start, ray_length, pixel_of_ray, observed):
    width_y = scalar.shape[1]
    rays_all = weights.shape[0]
    groups = lax.axis_size("gy")
    total_y = width_y * groups
    field = scalar
    saved = []
    for section in range(STEPS):
        padded = surround(field)
        saved.append(padded)
        centre, east, west, north, south, upper, lower = neighbours(padded)
        laplace = east + west + north + south + upper + lower - 6.0 * centre
        advect = (
            velocity[0] * (0.5 * (east - west))
            + velocity[1] * (0.5 * (north - south))
            + velocity[2] * (0.5 * (upper - lower))
        )
        field = centre + time_step * (diffusion * laplace - advect)
    scores = jnp.einsum(
        "xyz,rz->xyr",
        field,
        weights,
        precision=lax.Precision.HIGHEST,
        preferred_element_type=jnp.float32,
    )
    rows_here = lax.axis_index("gy") * width_y + jnp.arange(width_y, dtype=jnp.int32)
    ray_mask = (
        jnp.mod(rows_here[None, :, None] - ray_start[:, None, :], total_y) < ray_length[:, None, :]
    ).astype(jnp.float32)
    partial_value = jnp.sum(ray_mask * scores, axis=1)
    by_pixel = jnp.zeros_like(partial_value).at[:, pixel_of_ray].set(partial_value)
    block = rays_all // groups
    offset = lax.axis_index("gy") * block
    depth = lax.psum_scatter(by_pixel, "gy", scatter_dimension=1, tiled=True)
    images = jnp.exp(-depth)
    own_observed = lax.dynamic_slice_in_dim(observed, offset, block, 1)
    sensitivity_block = -(images - own_observed) * images
    sensitivity = lax.all_gather(sensitivity_block, "gy", axis=1, tiled=True)
    sensitivity_ray = sensitivity[:, pixel_of_ray]
    adjoint = jnp.einsum(
        "xyr,rz->xyz",
        ray_mask * sensitivity_ray[:, None, :],
        weights,
        precision=lax.Precision.HIGHEST,
        preferred_element_type=jnp.float32,
    )
    gradient_sum = jnp.zeros(velocity.shape, jnp.float32)
    for section in reversed(range(STEPS)):
        unused, east, west, north, south, upper, lower = neighbours(saved[section])
        slopes = jnp.stack([0.5 * (east - west), 0.5 * (north - south), 0.5 * (upper - lower)])
        gradient_sum = gradient_sum - time_step * adjoint[None] * slopes
        stacked = jnp.concatenate([adjoint[None], velocity * adjoint[None]], 0)
        padded = with_halo(stacked, (("gx", 1), ("gy", 2)), 1)
        centre, east, west, north, south, upper, lower = neighbours(padded)
        laplace = east[0] + west[0] + north[0] + south[0] + upper[0] + lower[0] - 6.0 * centre[0]
        transport = (
            0.5 * (east[1] - west[1]) + 0.5 * (north[2] - south[2]) + 0.5 * (upper[3] - lower[3])
        )
        adjoint = centre[0] + time_step * (diffusion * laplace + transport)
    return (images, adjoint, gradient_sum)


def solution(mesh):
    in_specs = (
        P("gx", "gy", None),
        P(None, "gx", "gy", None),
        P(),
        P("gx", None),
        P("gx", None),
        P(),
        P("gx", None),
    )
    out_specs = (P("gx", "gy"), P("gx", "gy", None), P(None, "gx", "gy", None))
    return jax.shard_map(
        per_device, mesh=mesh, in_specs=in_specs, out_specs=out_specs, check_vma=False
    )
```

profile of v0, /device:TPU:28, one launch (start us, length us, event | category | flops | bytes accessed | tf_op | source)
XLA Modules:
  0.0 178.5 jit_solution(4548214291667548617)
XLA Ops:
  8.4 1.7 collective-permute-start
  10.2 2.6 %collective-permute-done.1 = f32[1,128,256]{2,1,0:T(8,128)S(1)} collective-permute-done((f32[1,128,256]{2,1,0:T(8,128)S(1)}, f32[1,128,256]{2,1,0:T(8,128)S(1)}, u32[]{:S(2)}, u32[]{:S(2)}) %collective-permute-start.1) | collective-permute-done | bytes 131104 | tf_op jit(solution)/shard_map/ppermute | solution.py:20
  13.2 3.2 %fusion.86 = (f32[1,8,128,256]{3,2,1,0:T(8,128)}, f32[10,128,256]{2,1,0:T(8,128)S(1)}) fusion(f32[1,128,256]{2,1,0:T(8,128)S(1)} %collective-permute-done, f32[8,128,256]{2,1,0:T(8,128)} %param.7, f32[1,128,256]{2,1,0:T(8,128)S(1)} %collective-permute-done.1, f32[10,128,256]{2,1,0:T(8,128)S(1)} %constant_dynamic-update-slice_fusion.2), kind=kLoop, calls=%fused_computation.193 | loop fusion | flops 1048576 | bytes 3407872 | tf_op jit(solution)/shard_map/stack | solution.py:99
  16.4 1.6 collective-permute-start.3
  18.9 1.3 collective-permute-done.3
  20.2 1.5 collective-permute-done.2
  21.7 1.9 %fusion.82 = (f32[1,8,128,256]{3,2,1,0:T(8,128)}, f32[8,128,256]{2,1,0:T(8,128)S(1)}) fusion(f32[8,128,255]{2,1,0:T(8,128)S(1)} %get-tuple-element.50, f32[8,128,255]{2,1,0:T(8,128)S(1)} %get-tuple-element.49, f32[8,128,256]{2,1,0:T(8,128)S(1)} %copy-done.11, f32[3,8,128,256]{3,2,1,0:T(8,128)S(1)} %copy-done.2, ...), kind=kLoop, calls=%fused_computation.189 | loop fusion | flops 6553600 | bytes 9973760 | tf_op jit(solution)/shard_map/stack | solution.py:99
  23.7 1.2 collective-permute-start.5
  25.5 2.6 %collective-permute-done.5 = f32[1,128,256]{2,1,0:T(8,128)S(1)} collective-permute-done((f32[1,128,256]{2,1,0:T(8,128)S(1)}, f32[1,128,256]{2,1,0:T(8,128)S(1)}, u32[]{:S(2)}, u32[]{:S(2)}) %collective-permute-start.5) | collective-permute-done | bytes 131104 | tf_op jit(solution)/shard_map/ppermute | solution.py:20
  29.7 1.5 collective-permute-start.6
  31.5 1.3 collective-permute-done.7
  33.3 1.5 fusion.61
  35.7 3.0 %collective-permute-start.9 = (f32[1,128,256]{2,1,0:T(8,128)}, f32[1,128,256]{2,1,0:T(8,128)S(1)}, u32[]{:S(2)}, u32[]{:S(2)}) collective-permute-start(f32[1,128,256]{2,1,0:T(8,128)} %get-tuple-element.39), channel_id=1, source_target_pairs={{0,2},{2,4},{4,6},{6,8},{8,10},{10,12},{12,14},{14,16},{16,18},{18... | collective-permute-start | bytes 393224 | tf_op jit(solution)/shard_map/ppermute | solution.py:20
  40.4 1.2 collective-permute-done.8
  42.2 1.7 collective-permute-start.11
  44.7 1.3 collective-permute-done.11
  46.0 1.6 collective-permute-done.10
  47.6 9.2 %select_reduce_fusion = f32[8,1024]{1,0:T(8,128)} fusion(s32[8,1024]{1,0:T(8,128)S(1)} %copy-done.42, s32[8,1024]{1,0:T(8,128)S(1)} %copy-done.43, s32[128]{0:T(128)S(1)} %iota_add_fusion, f32[1024,256]{1,0:T(8,128)S(1)} %copy-done, f32[8,128,256]{2,1,0:T(8,128)S(1)} %fusion.61, f32[8,128,255]{2,1,0:T(8,128)S(1)} %get-tuple-element.42, ...), kind=kOutput, calls=%fused_computation.18 | convolution fusion | flops 3244548096 | bytes 7713280 | tf_op jit(solution)/shard_map/xyz,rz->xyr/dot_general | solution.py:68
  57.9 4.0 %scatter_custom_fusion = f32[8,1024]{0,1:T(8,128)} fusion(s32[1024]{0:T(1024)} %get-tuple-element.54, f32[1024,8]{1,0:T(8,128)S(1)} %copy.13, f32[]{:T(128)} %constant.11.clone.1), kind=kCustom, calls=%fused_computation.213 | custom fusion | bytes 33280 | tf_op jit(solution)/shard_map/scatter | solution.py:80
  62.7 18.1 %reduce-scatter.2.cloned.1.call-done = f32[8,512]{0,1:T(8,128)} async-done(((f32[8,1024]{0,1:T(8,128)}), f32[8,512]{0,1:T(8,128)}) %reduce-scatter.2.cloned.1.call-update) | async-done | bytes 16400 | tf_op jit(solution)/shard_map/reduce_scatter | solution.py:83
  80.8 1.7 negate_multiply_fusion
  82.5 8.9 %all_gather.3 = f32[8,1024]{0,1:T(8,128)S(1)} all-gather(f32[8,512]{0,1:T(8,128)S(1)} %get-tuple-element.51), channel_id=1, replica_groups=mesh['gx'=16,'gy'=2] {'gy'}, dimensions={1}, use_global_device_ids=true | all-gather | bytes 49152 | tf_op jit(solution)/shard_map/all_gather | solution.py:87
  91.4 2.8 %gather_fusion = f32[1024,8]{1,0:T(8,128)S(1)} fusion(f32[8,1024]{0,1:T(8,128)S(1)} %all_gather.3, s32[1024]{0:T(1024)S(1)} %get-tuple-element.53), kind=kCustom, calls=%fused_computation | custom fusion | bytes 69632 | tf_op jit(solution)/shard_map/gather | solution.py:88
  94.4 7.0 %broadcast_multiply_fusion.5 = (f32[8,128,256]{2,1,0:T(8,128)}, f32[8,128,256]{2,1,0:T(8,128)S(1)}) fusion(f32[1024,256]{1,0:T(8,128)S(1)} %copy-done, f32[8,1024]{1,0:T(8,128)S(1)} %copy.15, s32[8,1024]{1,0:T(8,128)} %param.11, s32[8,1024]{1,0:T(8,128)} %param.10, s32[128]{0:T(128)} %copy-done.44), kind=kOutput, calls=%fused_computation.205 | convolution fusion | flops 3236167680 | bytes 3244544 | tf_op jit(solution)/shard_map/xyr,rz->xyz/dot_general | solution.py:89
  102.0 1.7 collective-permute-start.12
  103.7 1.7 fusion.81
  105.4 1.1 select_maximum_fusion.2
  106.6 9.6 %collective-permute-done.13 = f32[4,1,128,256]{3,2,1,0:T(8,128)S(1)} collective-permute-done((f32[4,1,128,256]{3,2,1,0:T(8,128)S(1)}, f32[4,1,128,256]{3,2,1,0:T(8,128)S(1)}, u32[]{:S(2)}, u32[]{:S(2)}) %collective-permute-start.13) | collective-permute-done | bytes 524320 | tf_op jit(solution)/shard_map/ppermute | solution.py:20
  116.9 1.5 collective-permute-start.15
  120.9 2.3 %broadcast_multiply_fusion.4 = (f32[8,128,256]{2,1,0:T(8,128)}, f32[8,128,256]{2,1,0:T(8,128)S(1)}) fusion(f32[8,128,256]{2,1,0:T(8,128)S(1)} %get-tuple-element.56, f32[4,8,128,256]{3,2,1,0:T(8,128)S(1)} %select_maximum_fusion.2, f32[4,1,128,256]{3,2,1,0:T(8,128)S(1)} %collective-permute-done.12, f32[3,8,128,256]{3,2,1,0:T(8,128)S(1)} %broadcast_multiply_fusion.2, ...), kind=kLoop, calls=%fused_computation.204 | loop fusion | flops 10747904 | bytes 14745600 | tf_op jit(solution)/shard_map/mul | solution.py:100
  124.2 1.1 pad_maximum_fusion.60
  125.4 1.7 collective-permute-start.16
  127.1 1.6 fusion.87
  128.7 1.4 fusion.79
  130.2 2.6 %fusion.88 = (f32[1,8,128,256]{3,2,1,0:T(8,128)}, f32[1,8,128,256]{3,2,1,0:T(8,128)}) fusion(f32[1,128,256]{2,1,0:T(8,128)} %collective-permute-done.8, f32[8,128,256]{2,1,0:T(8,128)S(1)} %copy-done.10, f32[1,128,256]{2,1,0:T(8,128)S(1)} %collective-permute-done.9, f32[10,1,256]{2,1,0:T(1,128)S(1)} %copy-done.38, f32[10,1,256]{2,1,0:T(1,128)S(1)} %copy-done.40), kind=kLoop, calls=%fused_computation.195 | loop fusion | flops 3145728 | bytes 3428352 | tf_op jit(solution)/shard_map/stack | solution.py:99
  132.8 1.7 copy.16
  134.4 2.5 %select_maximum_fusion.1 = f32[4,8,128,256]{3,2,1,0:T(8,128)S(1)} fusion(f32[3,8,128,256]{3,2,1,0:T(8,128)S(1)} %broadcast_multiply_fusion.1, f32[1,8,128,256]{3,2,1,0:T(8,128)} %bitcast.135), kind=kLoop, calls=%fused_computation.11 | loop fusion | flops 4194304 | bytes 8388608 | tf_op jit(solution)/shard_map/concatenate | solution.py:101
  136.9 3.0 %collective-permute-done.17 = f32[4,1,128,256]{3,2,1,0:T(8,128)} collective-permute-done((f32[4,1,128,256]{3,2,1,0:T(8,128)}, f32[4,1,128,256]{3,2,1,0:T(8,128)}, u32[]{:S(2)}, u32[]{:S(2)}) %collective-permute-start.17) | collective-permute-done | bytes 524320 | tf_op jit(solution)/shard_map/ppermute | solution.py:20
  140.8 1.5 collective-permute-start.18
  142.9 1.2 slice_maximum_fusion.1
  144.9 1.5 collective-permute-done.19
  146.3 2.3 %broadcast_multiply_fusion.3 = (f32[8,128,256]{2,1,0:T(8,128)S(1)}, f32[8,128,256]{2,1,0:T(8,128)S(1)}) fusion(f32[8,128,256]{2,1,0:T(8,128)S(1)} %copy-done.6, f32[4,8,128,256]{3,2,1,0:T(8,128)S(1)} %select_maximum_fusion.1, f32[4,1,128,256]{3,2,1,0:T(8,128)} %collective-permute-done.16, f32[3,8,128,256]{3,2,1,0:T(8,128)S(1)} %broadcast_multiply_fusion.1, ...), kind=kLoop, calls=%fused_computation.203 | loop fusion | flops 10747904 | bytes 14745600 | tf_op jit(solution)/shard_map/mul | solution.py:100
  149.3 1.1 select_maximum_fusion
  150.5 1.7 collective-permute-start.20
  153.4 2.2 %fusion.6 = f32[3,8,128,256]{3,2,1,0:T(8,128)} fusion(f32[1,8,128,256]{3,2,1,0:T(8,128)S(1)} %copy-done.22, f32[1,8,128,256]{3,2,1,0:T(8,128)S(1)} %copy-done.29, f32[1,8,128,256]{3,2,1,0:T(8,128)S(1)} %copy-done.28, f32[1,8,128,256]{3,2,1,0:T(8,128)S(1)} %copy-done.24, f32[1,8,128,256]{3,2,1,0:T(8,128)S(1)} %copy-done.27, ...), kind=kLoop, calls=%fused_computation.28 | loop fusion | flops 9437184 | bytes 15728640 | tf_op jit(solution)/shard_map/sub | solution.py:100
  155.6 9.1 %collective-permute-done.21 = f32[4,1,128,256]{3,2,1,0:T(8,128)S(1)} collective-permute-done((f32[4,1,128,256]{3,2,1,0:T(8,128)S(1)}, f32[4,1,128,256]{3,2,1,0:T(8,128)S(1)}, u32[]{:S(2)}, u32[]{:S(2)}) %collective-permute-start.21) | collective-permute-done | bytes 524320 | tf_op jit(solution)/shard_map/ppermute | solution.py:20
  165.4 1.5 collective-permute-start.23
  169.4 2.3 %fusion.38 = f32[8,128,256]{2,1,0:T(8,128)} fusion(f32[8,128,256]{2,1,0:T(8,128)S(1)} %get-tuple-element.12, f32[4,8,128,255]{3,2,1,0:T(8,128)S(1)} %slice_maximum_fusion, f32[4,8,128,256]{3,2,1,0:T(8,128)S(1)} %select_maximum_fusion, f32[4,10,1,256]{3,2,1,0:T(1,128)S(1)} %collective-permute-done.23, f32[4,1,128,256]{3,2,1,0:T(8,128)S(1)} %collective-permute-done.20, ...), kind=kLoop, calls=%fused_computation.64 | loop fusion | flops 10485760 | bytes 13697024 | tf_op jit(solution)/shard_map/add | solution.py:108
  (143 shorter events, 23.4 us)
Async XLA Ops:
  7.2 40.5 %copy-start = (f32[1024,256]{1,0:T(8,128)S(1)}, f32[1024,256]{1,0:T(8,128)}, u32[]{:S(2)}) copy-start(f32[1024,256]{1,0:T(8,128)} %param.9) | copy-start | bytes 3145732
  7.2 11.3 %copy-start.11 = (f32[8,128,256]{2,1,0:T(8,128)S(1)}, f32[8,128,256]{2,1,0:T(8,128)}, u32[]{:S(2)}) copy-start(f32[8,128,256]{2,1,0:T(8,128)} %param.7) | copy-start | bytes 3145732
  7.2 73.6 %reduce-scatter.2.cloned.1.call-start = ((), (), s32[]{:S(2)}) async-start(), calls=%async_computation.1 | async-start | bytes 786432 | tf_op jit(solution)/shard_map/reduce_scatter | solution.py:83
  8.4 13.3 %copy-start.2 = (f32[3,8,128,256]{3,2,1,0:T(8,128)S(1)}, f32[3,8,128,256]{3,2,1,0:T(8,128)}, u32[]{:S(2)}) copy-start(f32[3,8,128,256]{3,2,1,0:T(8,128)} %param.8) | copy-start | bytes 9437188
  8.4 4.4 %collective-permute-start.1 = (f32[1,128,256]{2,1,0:T(8,128)S(1)}, f32[1,128,256]{2,1,0:T(8,128)S(1)}, u32[]{:S(2)}, u32[]{:S(2)}) collective-permute-start(f32[1,128,256]{2,1,0:T(8,128)S(1)} %get-tuple-element.47), channel_id=1, source_target_pairs={{0,2},{2,4},{4,6},{6,8},{8,10},{10,12},{12,14},{14,16},{16,18},{18... | collective-permute-start | bytes 393224 | tf_op jit(solution)/shard_map/ppermute | solution.py:20
  8.4 4.7 %collective-permute-start = (f32[1,128,256]{2,1,0:T(8,128)S(1)}, f32[1,128,256]{2,1,0:T(8,128)S(1)}, u32[]{:S(2)}, u32[]{:S(2)}) collective-permute-start(f32[1,128,256]{2,1,0:T(8,128)S(1)} %get-tuple-element.48), channel_id=1, source_target_pairs={{2,0},{4,2},{6,4},{8,6},{10,8},{12,10},{14,12},{16,14},{18,16},{20... | collective-permute-start | bytes 393224 | tf_op jit(solution)/shard_map/ppermute | solution.py:22
  16.4 7.3 %copy-start.14 = (f32[10,128,256]{2,1,0:T(8,128)}, f32[10,128,256]{2,1,0:T(8,128)S(1)}, u32[]{:S(2)}) copy-start(f32[10,128,256]{2,1,0:T(8,128)S(1)} %constant_dynamic-update-slice_fusion) | copy-start | bytes 3932164
  16.4 3.7 %collective-permute-start.3 = (f32[10,1,256]{2,1,0:T(1,128)S(1)}, f32[10,1,256]{2,1,0:T(1,128)S(1)}, u32[]{:S(2)}, u32[]{:S(2)}) collective-permute-start(f32[10,1,256]{2,1,0:T(1,128)S(1)} %get-tuple-element.35), channel_id=1, source_target_pairs={{0,1},{1,0},{2,3},{3,2},{4,5},{5,4},{6,7},{7,6},{8,9},{9,8},{10,11... | collective-permute-start | bytes 30728 | tf_op jit(solution)/shard_map/ppermute | solution.py:20
  18.0 3.7 %collective-permute-start.2 = (f32[10,1,256]{2,1,0:T(1,128)S(1)}, f32[10,1,256]{2,1,0:T(1,128)S(1)}, u32[]{:S(2)}, u32[]{:S(2)}) collective-permute-start(f32[10,1,256]{2,1,0:T(1,128)S(1)} %get-tuple-element.36), channel_id=1, source_target_pairs={{1,0},{0,1},{3,2},{2,3},{5,4},{4,5},{7,6},{6,7},{9,8},{8,9},{11,10... | collective-permute-start | bytes 30728 | tf_op jit(solution)/shard_map/ppermute | solution.py:22
  23.6 11.2 %copy-start.7 = (f32[8,128,256]{2,1,0:T(8,128)}, f32[8,128,256]{2,1,0:T(8,128)S(1)}, u32[]{:S(2)}) copy-start(f32[8,128,256]{2,1,0:T(8,128)S(1)} %get-tuple-element.26) | copy-start | bytes 3145732
  23.7 4.4 %collective-permute-start.5 = (f32[1,128,256]{2,1,0:T(8,128)S(1)}, f32[1,128,256]{2,1,0:T(8,128)S(1)}, u32[]{:S(2)}, u32[]{:S(2)}) collective-permute-start(f32[1,128,256]{2,1,0:T(8,128)S(1)} %get-tuple-element.43), channel_id=1, source_target_pairs={{0,2},{2,4},{4,6},{6,8},{8,10},{10,12},{12,14},{14,16},{16,18},{18... | collective-permute-start | bytes 393224 | tf_op jit(solution)/shard_map/ppermute | solution.py:20
  24.9 4.2 %collective-permute-start.4 = (f32[1,128,256]{2,1,0:T(8,128)S(1)}, f32[1,128,256]{2,1,0:T(8,128)S(1)}, u32[]{:S(2)}, u32[]{:S(2)}) collective-permute-start(f32[1,128,256]{2,1,0:T(8,128)S(1)} %get-tuple-element.44), channel_id=1, source_target_pairs={{2,0},{4,2},{6,4},{8,6},{10,8},{12,10},{14,12},{16,14},{18,16},{20... | collective-permute-start | bytes 393224 | tf_op jit(solution)/shard_map/ppermute | solution.py:22
  29.1 3.7 %collective-permute-start.7 = (f32[10,1,256]{2,1,0:T(1,128)S(1)}, f32[10,1,256]{2,1,0:T(1,128)S(1)}, u32[]{:S(2)}, u32[]{:S(2)}) collective-permute-start(f32[10,1,256]{2,1,0:T(1,128)S(1)} %get-tuple-element.33), channel_id=1, source_target_pairs={{0,1},{1,0},{2,3},{3,2},{4,5},{5,4},{6,7},{7,6},{8,9},{9,8},{10,11... | collective-permute-start | bytes 30728 | tf_op jit(solution)/shard_map/ppermute | solution.py:20
  29.7 3.7 %collective-permute-start.6 = (f32[10,1,256]{2,1,0:T(1,128)S(1)}, f32[10,1,256]{2,1,0:T(1,128)S(1)}, u32[]{:S(2)}, u32[]{:S(2)}) collective-permute-start(f32[10,1,256]{2,1,0:T(1,128)S(1)} %get-tuple-element.34), channel_id=1, source_target_pairs={{1,0},{0,1},{3,2},{2,3},{5,4},{4,5},{7,6},{6,7},{9,8},{8,9},{11,10... | collective-permute-start | bytes 30728 | tf_op jit(solution)/shard_map/ppermute | solution.py:22
  31.5 7.2 %copy-start.41 = (s32[1024]{0:T(1024)S(1)}, s32[1024]{0:T(1024)}, u32[]{:S(2)}) copy-start(s32[1024]{0:T(1024)} %param.12) | copy-start | bytes 12292
  34.9 22.0 %copy-start.9 = (f32[8,128,256]{2,1,0:T(8,128)}, f32[8,128,256]{2,1,0:T(8,128)S(1)}, u32[]{:S(2)}) copy-start(f32[8,128,256]{2,1,0:T(8,128)S(1)} %fusion.61) | copy-start | bytes 3145732
  35.7 4.7 %collective-permute-start.9 = (f32[1,128,256]{2,1,0:T(8,128)}, f32[1,128,256]{2,1,0:T(8,128)S(1)}, u32[]{:S(2)}, u32[]{:S(2)}) collective-permute-start(f32[1,128,256]{2,1,0:T(8,128)} %get-tuple-element.39), channel_id=1, source_target_pairs={{0,2},{2,4},{4,6},{6,8},{8,10},{10,12},{12,14},{14,16},{16,18},{18... | collective-permute-start | bytes 393224 | tf_op jit(solution)/shard_map/ppermute | solution.py:20
  38.7 2.8 %collective-permute-start.8 = (f32[1,128,256]{2,1,0:T(8,128)}, f32[1,128,256]{2,1,0:T(8,128)}, u32[]{:S(2)}, u32[]{:S(2)}) collective-permute-start(f32[1,128,256]{2,1,0:T(8,128)} %get-tuple-element.40), channel_id=1, source_target_pairs={{2,0},{4,2},{6,4},{8,6},{10,8},{12,10},{14,12},{16,14},{18,16},{20... | collective-permute-start | bytes 393224 | tf_op jit(solution)/shard_map/ppermute | solution.py:22
  39.3 8.4 %copy-start.42 = (s32[8,1024]{1,0:T(8,128)S(1)}, s32[8,1024]{1,0:T(8,128)}, u32[]{:S(2)}) copy-start(s32[8,1024]{1,0:T(8,128)} %param.11) | copy-start | bytes 98308
  39.3 8.4 %copy-start.43 = (s32[8,1024]{1,0:T(8,128)S(1)}, s32[8,1024]{1,0:T(8,128)}, u32[]{:S(2)}) copy-start(s32[8,1024]{1,0:T(8,128)} %param.10) | copy-start | bytes 98308
  39.3 17.6 %copy-start.44 = (s32[128]{0:T(128)}, s32[128]{0:T(128)S(1)}, u32[]{:S(2)}) copy-start(s32[128]{0:T(128)S(1)} %iota_add_fusion) | copy-start | bytes 1540
  42.2 3.7 %collective-permute-start.11 = (f32[10,1,256]{2,1,0:T(1,128)S(1)}, f32[10,1,256]{2,1,0:T(1,128)S(1)}, u32[]{:S(2)}, u32[]{:S(2)}) collective-permute-start(f32[10,1,256]{2,1,0:T(1,128)S(1)} %get-tuple-element.31), channel_id=1, source_target_pairs={{0,1},{1,0},{2,3},{3,2},{4,5},{5,4},{6,7},{7,6},{8,9},{9,8},{10,11... | collective-permute-start | bytes 30728 | tf_op jit(solution)/shard_map/ppermute | solution.py:20
  44.0 3.7 %collective-permute-start.10 = (f32[10,1,256]{2,1,0:T(1,128)S(1)}, f32[10,1,256]{2,1,0:T(1,128)S(1)}, u32[]{:S(2)}, u32[]{:S(2)}) collective-permute-start(f32[10,1,256]{2,1,0:T(1,128)S(1)} %get-tuple-element.32), channel_id=1, source_target_pairs={{1,0},{0,1},{3,2},{2,3},{5,4},{4,5},{7,6},{6,7},{9,8},{8,9},{11,10... | collective-permute-start | bytes 30728 | tf_op jit(solution)/shard_map/ppermute | solution.py:22
  44.7 12.2 %copy-start.16 = (f32[8,128,255]{2,1,0:T(8,128)}, f32[8,128,255]{2,1,0:T(8,128)S(1)}, u32[]{:S(2)}) copy-start(f32[8,128,255]{2,1,0:T(8,128)S(1)} %get-tuple-element.41) | copy-start | bytes 3133444
  44.7 12.2 %copy-start.18 = (f32[8,128,255]{2,1,0:T(8,128)}, f32[8,128,255]{2,1,0:T(8,128)S(1)}, u32[]{:S(2)}) copy-start(f32[8,128,255]{2,1,0:T(8,128)S(1)} %get-tuple-element.42) | copy-start | bytes 3133444
  46.0 10.9 %copy-start.37 = (f32[10,1,256]{2,1,0:T(1,128)}, f32[10,1,256]{2,1,0:T(1,128)S(1)}, u32[]{:S(2)}) copy-start(f32[10,1,256]{2,1,0:T(1,128)S(1)} %collective-permute-done.11) | copy-start | bytes 30724
  47.6 9.3 %copy-start.39 = (f32[10,1,256]{2,1,0:T(1,128)}, f32[10,1,256]{2,1,0:T(1,128)S(1)}, u32[]{:S(2)}) copy-start(f32[10,1,256]{2,1,0:T(1,128)S(1)} %collective-permute-done.10) | copy-start | bytes 30724
  94.4 7.0 %copy-start.3 = (f32[3,8,128,256]{3,2,1,0:T(8,128)S(1)}, f32[3,8,128,256]{3,2,1,0:T(8,128)}, u32[]{:S(2)}) copy-start(f32[3,8,128,256]{3,2,1,0:T(8,128)} %param.8) | copy-start | bytes 9437188
  101.9 14.3 %collective-permute-start.13 = (f32[4,1,128,256]{3,2,1,0:T(8,128)S(1)}, f32[4,1,128,256]{3,2,1,0:T(8,128)S(1)}, u32[]{:S(2)}, u32[]{:S(2)}) collective-permute-start(f32[4,1,128,256]{3,2,1,0:T(8,128)S(1)} %get-tuple-element.23), channel_id=1, source_target_pairs={{0,2},{2,4},{4,6},{6,8},{8,10},{10,12},{12,14},{14,16},{16,18},{18... | collective-permute-start | bytes 1572872 | tf_op jit(solution)/shard_map/ppermute | solution.py:20
  102.0 14.2 %collective-permute-start.12 = (f32[4,1,128,256]{3,2,1,0:T(8,128)S(1)}, f32[4,1,128,256]{3,2,1,0:T(8,128)S(1)}, u32[]{:S(2)}, u32[]{:S(2)}) collective-permute-start(f32[4,1,128,256]{3,2,1,0:T(8,128)S(1)} %get-tuple-element.24), channel_id=1, source_target_pairs={{2,0},{4,2},{6,4},{8,6},{10,8},{12,10},{14,12},{16,14},{18,16},{20... | collective-permute-start | bytes 1572872 | tf_op jit(solution)/shard_map/ppermute | solution.py:22
  116.2 4.1 %collective-permute-start.14 = (f32[4,10,1,256]{3,2,1,0:T(1,128)S(1)}, f32[4,10,1,256]{3,2,1,0:T(1,128)S(1)}, u32[]{:S(2)}, u32[]{:S(2)}) collective-permute-start(f32[4,10,1,256]{3,2,1,0:T(1,128)S(1)} %get-tuple-element.17), channel_id=1, source_target_pairs={{1,0},{0,1},{3,2},{2,3},{5,4},{4,5},{7,6},{6,7},{9,8},{8,9},{11,10... | collective-permute-start | bytes 122888 | tf_op jit(solution)/shard_map/ppermute | solution.py:22
  116.9 4.0 %collective-permute-start.15 = (f32[4,10,1,256]{3,2,1,0:T(1,128)S(1)}, f32[4,10,1,256]{3,2,1,0:T(1,128)S(1)}, u32[]{:S(2)}, u32[]{:S(2)}) collective-permute-start(f32[4,10,1,256]{3,2,1,0:T(1,128)S(1)} %get-tuple-element.18), channel_id=1, source_target_pairs={{0,1},{1,0},{2,3},{3,2},{4,5},{5,4},{6,7},{7,6},{8,9},{9,8},{10,11... | collective-permute-start | bytes 122888 | tf_op jit(solution)/shard_map/ppermute | solution.py:20
  124.2 4.5 %copy-start.17 = (f32[8,128,255]{2,1,0:T(8,128)S(1)}, f32[8,128,255]{2,1,0:T(8,128)}, u32[]{:S(2)}) copy-start(f32[8,128,255]{2,1,0:T(8,128)} %copy-done.16) | copy-start | bytes 3133444
  124.2 4.5 %copy-start.19 = (f32[8,128,255]{2,1,0:T(8,128)S(1)}, f32[8,128,255]{2,1,0:T(8,128)}, u32[]{:S(2)}) copy-start(f32[8,128,255]{2,1,0:T(8,128)} %copy-done.18) | copy-start | bytes 3133444
  125.4 4.8 %copy-start.10 = (f32[8,128,256]{2,1,0:T(8,128)S(1)}, f32[8,128,256]{2,1,0:T(8,128)}, u32[]{:S(2)}) copy-start(f32[8,128,256]{2,1,0:T(8,128)} %copy-done.9) | copy-start | bytes 3145732
  125.4 4.8 %copy-start.38 = (f32[10,1,256]{2,1,0:T(1,128)S(1)}, f32[10,1,256]{2,1,0:T(1,128)}, u32[]{:S(2)}) copy-start(f32[10,1,256]{2,1,0:T(1,128)} %copy-done.37) | copy-start | bytes 30724
  125.4 4.8 %copy-start.40 = (f32[10,1,256]{2,1,0:T(1,128)S(1)}, f32[10,1,256]{2,1,0:T(1,128)}, u32[]{:S(2)}) copy-start(f32[10,1,256]{2,1,0:T(1,128)} %copy-done.39) | copy-start | bytes 30724
  125.4 14.5 %collective-permute-start.17 = (f32[4,1,128,256]{3,2,1,0:T(8,128)}, f32[4,1,128,256]{3,2,1,0:T(8,128)}, u32[]{:S(2)}, u32[]{:S(2)}) collective-permute-start(f32[4,1,128,256]{3,2,1,0:T(8,128)} %get-tuple-element.21), channel_id=1, source_target_pairs={{0,2},{2,4},{4,6},{6,8},{8,10},{10,12},{12,14},{14,16},{16,18},{18... | collective-permute-start | bytes 1572872 | tf_op jit(solution)/shard_map/ppermute | solution.py:20
  125.4 14.5 %collective-permute-start.16 = (f32[4,1,128,256]{3,2,1,0:T(8,128)}, f32[4,1,128,256]{3,2,1,0:T(8,128)}, u32[]{:S(2)}, u32[]{:S(2)}) collective-permute-start(f32[4,1,128,256]{3,2,1,0:T(8,128)} %get-tuple-element.22), channel_id=1, source_target_pairs={{2,0},{4,2},{6,4},{8,6},{10,8},{12,10},{14,12},{16,14},{18,16},{20... | collective-permute-start | bytes 1572872 | tf_op jit(solution)/shard_map/ppermute | solution.py:22
  134.4 5.5 %copy-start.6 = (f32[8,128,256]{2,1,0:T(8,128)S(1)}, f32[8,128,256]{2,1,0:T(8,128)}, u32[]{:S(2)}) copy-start(f32[8,128,256]{2,1,0:T(8,128)} %copy-done.5) | copy-start | bytes 3145732
  140.8 4.1 %collective-permute-start.18 = (f32[4,10,1,256]{3,2,1,0:T(1,128)S(1)}, f32[4,10,1,256]{3,2,1,0:T(1,128)S(1)}, u32[]{:S(2)}, u32[]{:S(2)}) collective-permute-start(f32[4,10,1,256]{3,2,1,0:T(1,128)S(1)} %get-tuple-element.15), channel_id=1, source_target_pairs={{1,0},{0,1},{3,2},{2,3},{5,4},{4,5},{7,6},{6,7},{9,8},{8,9},{11,10... | collective-permute-start | bytes 122888 | tf_op jit(solution)/shard_map/ppermute | solution.py:22
  142.3 4.0 %collective-permute-start.19 = (f32[4,10,1,256]{3,2,1,0:T(1,128)S(1)}, f32[4,10,1,256]{3,2,1,0:T(1,128)S(1)}, u32[]{:S(2)}, u32[]{:S(2)}) collective-permute-start(f32[4,10,1,256]{3,2,1,0:T(1,128)S(1)} %get-tuple-element.16), channel_id=1, source_target_pairs={{0,1},{1,0},{2,3},{3,2},{4,5},{5,4},{6,7},{7,6},{8,9},{9,8},{10,11... | collective-permute-start | bytes 122888 | tf_op jit(solution)/shard_map/ppermute | solution.py:20
  144.1 4.6 %copy-start.4 = (f32[3,8,128,256]{3,2,1,0:T(8,128)S(1)}, f32[3,8,128,256]{3,2,1,0:T(8,128)}, u32[]{:S(2)}) copy-start(f32[3,8,128,256]{3,2,1,0:T(8,128)} %param.8) | copy-start | bytes 9437188
  150.4 14.3 %collective-permute-start.21 = (f32[4,1,128,256]{3,2,1,0:T(8,128)S(1)}, f32[4,1,128,256]{3,2,1,0:T(8,128)S(1)}, u32[]{:S(2)}, u32[]{:S(2)}) collective-permute-start(f32[4,1,128,256]{3,2,1,0:T(8,128)S(1)} %get-tuple-element.19), channel_id=1, source_target_pairs={{0,2},{2,4},{4,6},{6,8},{8,10},{10,12},{12,14},{14,16},{16,18},{18... | collective-permute-start | bytes 1572872 | tf_op jit(solution)/shard_map/ppermute | solution.py:20
  150.5 14.2 %collective-permute-start.20 = (f32[4,1,128,256]{3,2,1,0:T(8,128)S(1)}, f32[4,1,128,256]{3,2,1,0:T(8,128)S(1)}, u32[]{:S(2)}, u32[]{:S(2)}) collective-permute-start(f32[4,1,128,256]{3,2,1,0:T(8,128)S(1)} %get-tuple-element.20), channel_id=1, source_target_pairs={{2,0},{4,2},{6,4},{8,6},{10,8},{12,10},{14,12},{16,14},{18,16},{20... | collective-permute-start | bytes 1572872 | tf_op jit(solution)/shard_map/ppermute | solution.py:22
  164.7 4.1 %collective-permute-start.22 = (f32[4,10,1,256]{3,2,1,0:T(1,128)S(1)}, f32[4,10,1,256]{3,2,1,0:T(1,128)S(1)}, u32[]{:S(2)}, u32[]{:S(2)}) collective-permute-start(f32[4,10,1,256]{3,2,1,0:T(1,128)S(1)} %get-tuple-element.13), channel_id=1, source_target_pairs={{1,0},{0,1},{3,2},{2,3},{5,4},{4,5},{7,6},{6,7},{9,8},{8,9},{11,10... | collective-permute-start | bytes 122888 | tf_op jit(solution)/shard_map/ppermute | solution.py:22
  165.4 4.0 %collective-permute-start.23 = (f32[4,10,1,256]{3,2,1,0:T(1,128)S(1)}, f32[4,10,1,256]{3,2,1,0:T(1,128)S(1)}, u32[]{:S(2)}, u32[]{:S(2)}) collective-permute-start(f32[4,10,1,256]{3,2,1,0:T(1,128)S(1)} %get-tuple-element.14), channel_id=1, source_target_pairs={{0,1},{1,0},{2,3},{3,2},{4,5},{5,4},{6,7},{7,6},{8,9},{9,8},{10,11... | collective-permute-start | bytes 122888 | tf_op jit(solution)/shard_map/ppermute | solution.py:20
  166.8 4.9 %copy-start.1 = (f32[1024,256]{1,0:T(8,128)S(1)}, f32[1024,256]{1,0:T(8,128)}, u32[]{:S(2)}) copy-start(f32[1024,256]{1,0:T(8,128)} %param.9) | copy-start | bytes 3145732
  (22 other events, 65.3 us)
Sparse Core Ops, SparseCore 0:
  62.0 18.7 reduce-scatter.1
where the time goes:
time: 179 us
  waiting for transfers between devices  61.2 us (34%)
  other arithmetic  37.8 us (21%)
  starting transfers between devices  24.5 us (14%)
  matrix products  16.2 us (9%)
  local copies, waits for them, and re-layouts  15.5 us (9%)
  between operations  14.5 us (8%)
  blocking collectives  8.89 us (5%)
    ppermute x12, waiting for transfers between devices, with_halo(): lax.ppermute(tail, axis, [(i, (i + 1) % count) for i in range(count)])  34.5 us
    reduce_scatter x1, waiting for transfers between devices, per_device(): depth = lax.psum_scatter(by_pixel, 'gy', scatter_dimension=1, tiled=True)  18.1 us
    ppermute x12, starting transfers between devices, with_halo(): lax.ppermute(head, axis, [((i + 1) % count, i) for i in range(count)])  12.7 us
    another operation x6, other arithmetic, per_device(): jnp.stack([0.5 * (east - west), 0.5 * (north - south), 0.5 * (upper - low...  12.5 us
    ppermute x12, starting transfers between devices, with_halo(): lax.ppermute(tail, axis, [(i, (i + 1) % count) for i in range(count)])  11.7 us
    dot_general x1, matrix products, per_device(): jnp.einsum('xyz,rz->xyr', field, weights, precision=lax.Precision.HIGHEST...  9.24 us
    all_gather x1, blocking collectives, per_device(): sensitivity = lax.all_gather(sensitivity_block, 'gy', axis=1, tiled=True)  8.89 us
    ppermute x12, waiting for transfers between devices, with_halo(): lax.ppermute(head, axis, [((i + 1) % count, i) for i in range(count)])  8.53 us
  transfers between devices with their start and end apart: 25, of which 22 were waited for; matrix products, arithmetic and copies ran while one was open for 12% of the time, Pallas kernels for 0%

commit v1 on v0

v1 whole, which is shorter than its diff:
```python
import functools

import jax
import jax.numpy as jnp
from jax import lax
from jax.experimental import pallas as pl
from jax.experimental.pallas import tpu as pltpu
from jax.sharding import PartitionSpec as P

STEPS = 3
DT = 0.1
PAD = 8
MESH = pl.DeviceIdType.MESH
F32, BF16 = jnp.float32, jnp.bfloat16


def body(
    gx, gy,
    scalar, velocity, weights, start, length, pixel, observed,
    images, grad_scalar, grad_velocity,
    C, c3, vel, wf, wt, whi, wlo, mask, onehot, obs_ray, sens,
    A, PE, PW, PN, PS, cstage, crecv, astage, arecv, tau, taurecv,
    load_sem, xsend, xrecv, ysend, yrecv, tsend, trecv,
):
    nx, ny, nz = c3.shape
    rays = weights.shape[0]
    total_y = ny * gy
    block = rays // gy
    mx, my = lax.axis_index("gx"), lax.axis_index("gy")
    right, left = lax.rem(mx + 1, gx), lax.rem(mx + gx - 1, gx)
    north, south = lax.rem(my + 1, gy), lax.rem(my + gy - 1, gy)
    rows = pl.ds(PAD, ny)
    cut = 32

    local = [
        pltpu.make_async_copy(scalar, C.at[0, pl.ds(1, nx), rows], load_sem.at[0]),
        pltpu.make_async_copy(velocity, vel, load_sem.at[1]),
        pltpu.make_async_copy(weights, wf, load_sem.at[2]),
    ]
    for copy in local:
        copy.start()

    barrier = pltpu.get_barrier_semaphore()
    peers = [lax.rem(my + d, gy) for d in range(1, gy)]
    for who in (left, right):
        pl.semaphore_signal(barrier, inc=1, device_id=(who, my), device_id_type=MESH)
    for who in peers:
        pl.semaphore_signal(barrier, inc=1, device_id=(mx, who), device_id_type=MESH)
    pl.semaphore_wait(barrier, 2 + len(peers))

    def xcopies(k, to_right, at_right, to_left, at_left):
        return [
            pltpu.make_async_remote_copy(
                to_right, at_right, xsend.at[k, 0], xrecv.at[k, 0],
                device_id=(right, my), device_id_type=MESH),
            pltpu.make_async_remote_copy(
                to_left, at_left, xsend.at[k, 1], xrecv.at[k, 1],
                device_id=(left, my), device_id_type=MESH),
        ]

    def ycopies(k, stage, recv, n):
        return [
            pltpu.make_async_remote_copy(
                stage.at[n, 0], recv.at[n, 0], ysend.at[k, 0], yrecv.at[k, 0],
                device_id=(mx, north), device_id_type=MESH),
            pltpu.make_async_remote_copy(
                stage.at[n, 1], recv.at[n, 1], ysend.at[k, 1], yrecv.at[k, 1],
                device_id=(mx, south), device_id_type=MESH),
        ]

    cx, cy, ax, ay = [], [], [], []
    for n in range(STEPS):
        cx.append(xcopies(
            n,
            scalar.at[nx - 1] if n == 0 else C.at[n, nx, rows], C.at[n, 0, rows],
            scalar.at[0] if n == 0 else C.at[n, 1, rows], C.at[n, nx + 1, rows]))
        cy.append(ycopies(n, cstage, crecv, n))
        ax.append(xcopies(
            STEPS + n,
            PW.at[n, nx], PW.at[n, 0],
            PE.at[n, 0], PE.at[n, nx]))
        ay.append(ycopies(STEPS + n, astage, arecv, n))

    for copy in cx[0]:
        copy.start()

    def planes(lo, hi, f):
        lax.fori_loop(lo, hi, lambda i, x: (f(i), x)[1], 0)

    def edges(f):
        lax.fori_loop(0, 2, lambda t, x: (f(t * (nx - 1)), x)[1], 0)

    lane = lax.broadcasted_iota(jnp.int32, (cut, nz), 1)

    def shifts_z(up, down):
        upper = jnp.where(lane == nz - 1, 0.0, pltpu.roll(up, nz - 1, 1))
        lower = jnp.where(lane == 0, 0.0, pltpu.roll(down, 1, 1))
        return upper, lower

    def around(n, i, k):
        at = PAD + k * cut
        c = C[n, i + 1, pl.ds(at, cut), :]
        east = C[n, i + 2, pl.ds(at, cut), :]
        west = C[n, i, pl.ds(at, cut), :]
        up_y = C[n, i + 1, pl.ds(at + 1, cut), :]
        down_y = C[n, i + 1, pl.ds(at - 1, cut), :]
        upper, lower = shifts_z(c, c)
        return c, east, west, up_y, down_y, upper, lower

    def stage_c(n, i):
        cstage[n, 0, pl.ds(i, 1), :] = C[n, i + 1, pl.ds(PAD + ny - 1, 1), :]
        cstage[n, 1, pl.ds(i, 1), :] = C[n, i + 1, pl.ds(PAD, 1), :]

    def forward(n, i):
        for k in range(ny // cut):
            c, east, west, up_y, down_y, upper, lower = around(n, i, k)
            here = pl.ds(k * cut, cut)
            u, v, w = vel[0, i, here, :], vel[1, i, here, :], vel[2, i, here, :]
            lap = east + west + up_y + down_y + upper + lower - 6.0 * c
            adv = u * (east - west) + v * (up_y - down_y) + w * (upper - lower)
            new = c + DT * (lap - 0.5 * adv)
            if n < STEPS - 1:
                C[n + 1, i + 1, pl.ds(PAD + k * cut, cut), :] = new
            else:
                c3[i, here, :] = new
        if n < STEPS - 1:
            stage_c(n + 1, i)

    def make_mask(i):
        s, l = start[pl.ds(i, 1), :], length[pl.ds(i, 1), :]
        for k in range(ny // cut):
            y = my * ny + k * cut + lax.broadcasted_iota(jnp.int32, (cut, rays), 0)
            d = y - s
            d = jnp.where(d < 0, d + total_y, d)
            m = jnp.where(d < l, 1.0, 0.0).astype(BF16)
            mask[i, pl.ds(k * cut, cut), :] = m
            mask[i, pl.ds(ny + k * cut, cut), :] = m

    def make_onehot(k):
        size = 64
        p = k * size + lax.broadcasted_iota(jnp.int32, (size, rays), 0)
        onehot[pl.ds(pl.multiple_of(k * size, size), size), :] = jnp.where(
            p == pixel[...], 1.0, 0.0).astype(BF16)

    def pieces(x):
        a = x.astype(BF16).astype(F32)
        b = (x - a).astype(BF16).astype(F32)
        c = x - a - b
        return jnp.concatenate([a, b, c, jnp.zeros_like(x)], 0).astype(BF16)

    def gathered(y):
        return y[:nx] + y[nx:2 * nx] + y[2 * nx:3 * nx]

    def split_weights(k):
        size = 128
        at = pl.ds(pl.multiple_of(k * size, size), size)
        w = wf[at, :]
        hi = w.astype(BF16)
        whi[at, :] = hi
        wlo[at, :] = (w - hi.astype(F32)).astype(BF16)
        wt[:, at] = w.T

    def project(i):
        ct = c3[i].T
        hi = ct.astype(BF16)
        lo = (ct - hi.astype(F32)).astype(BF16)
        both = jnp.concatenate([hi, lo], 1)
        size = 256
        for k in range(rays // size):
            at = pl.ds(k * size, size)
            s = jnp.dot(both, mask[i, :, at], preferred_element_type=F32)
            tau[pl.ds(i, 1), at] = jnp.sum(s * wt[:, at], axis=0, keepdims=True)

    def spread(x):
        one = jnp.broadcast_to(x, (16, rays)).astype(BF16)
        return jnp.concatenate([one] * (ny // 16), 0)

    def products(n, i, k, a):
        here = pl.ds(k * cut, cut)
        u, v = vel[0, i, here, :], vel[1, i, here, :]
        ua, va = 0.5 * u * a, 0.5 * v * a
        A[n, i, here, :] = a
        PE[n, i, here, :] = a + ua
        PW[n, i + 1, here, :] = a - ua
        PN[n, i, pl.ds(PAD + k * cut, cut), :] = a + va
        PS[n, i, pl.ds(PAD + k * cut, cut), :] = a - va

    def stage_a(n, i):
        astage[n, 0, pl.ds(i, 1), :] = PS[n, i, pl.ds(PAD + ny - 1, 1), :]
        astage[n, 1, pl.ds(i, 1), :] = PN[n, i, pl.ds(PAD, 1), :]

    def back_project(t):
        his, los = [], []
        for i in (t, nx - 1 - t):
            s = sens[pl.ds(i, 1), :]
            hi = s.astype(BF16).astype(F32)
            m = mask[i, :ny, :]
            his.append(m * spread(hi))
            los.append(m * spread(s - hi))
        hi, lo = jnp.concatenate(his, 0), jnp.concatenate(los, 0)
        a = (jnp.dot(hi, whi[...], preferred_element_type=F32)
             + jnp.dot(lo, whi[...], preferred_element_type=F32)
             + jnp.dot(hi, wlo[...], preferred_element_type=F32))
        for j, i in enumerate((t, nx - 1 - t)):
            for k in range(ny // cut):
                products(0, i, k, a[j * ny + k * cut:j * ny + (k + 1) * cut])
            stage_a(0, i)

    def backward(n, i):
        for k in range(ny // cut):
            here = pl.ds(k * cut, cut)
            at = PAD + k * cut
            a = A[n, i, here, :]
            wa = 0.5 * vel[2, i, here, :] * a
            upper, lower = shifts_z(a + wa, a - wa)
            near = (PE[n, i + 1, here, :] + PW[n, i, here, :]
                    + PN[n, i, pl.ds(at + 1, cut), :] + PS[n, i, pl.ds(at - 1, cut), :]
                    + upper + lower)
            new = a + DT * (near - 6.0 * a)
            if n < STEPS - 1:
                products(n + 1, i, k, new)
            else:
                grad_scalar[i, here, :] = new
        if n < STEPS - 1:
            stage_a(n + 1, i)

    def slopes(n, m, i):
        for k in range(ny // cut):
            c, east, west, up_y, down_y, upper, lower = around(m, i, k)
            here = pl.ds(k * cut, cut)
            a = (-0.5 * DT) * A[n, i, here, :]
            for j, d in enumerate((east - west, up_y - down_y, upper - lower)):
                if n == 0:
                    grad_velocity[j, i, here, :] = a * d
                else:
                    grad_velocity[j, i, here, :] += a * d

    local[0].wait()
    planes(0, nx, functools.partial(stage_c, 0))
    for copy in cy[0]:
        copy.start()
    planes(0, nx, make_mask)
    local[1].wait()
    for n in range(STEPS):
        if n == 1:
            planes(0, rays // 64, make_onehot)
            g = jnp.dot(pieces(observed[...]), onehot[...], preferred_element_type=F32)
            obs_ray[...] = gathered(g)
            local[2].wait()
            planes(0, rays // 128, split_weights)
        for copy in cy[n]:
            copy.wait()
        for i in range(nx):
            C[n, i + 1, pl.ds(PAD - 1, 1), :] = crecv[n, 0, pl.ds(i, 1), :]
            C[n, i + 1, pl.ds(PAD + ny, 1), :] = crecv[n, 1, pl.ds(i, 1), :]
        planes(1, nx - 1, functools.partial(forward, n))
        if n == STEPS - 1:
            planes(1, nx - 1, project)
        for copy in cx[n]:
            copy.wait()
        edges(functools.partial(forward, n))
        if n < STEPS - 1:
            for copy in cx[n + 1] + cy[n + 1]:
                copy.start()
        else:
            edges(project)

    sends = [
        pltpu.make_async_remote_copy(
            tau, taurecv.at[d], tsend.at[d], trecv.at[d],
            device_id=(mx, who), device_id_type=MESH)
        for d, who in enumerate(peers)
    ]
    for copy in sends:
        copy.start()
    for copy in sends:
        copy.wait()
    depth = tau[...]
    for d in range(len(peers)):
        depth = depth + taurecv[d]
    img = jnp.exp(-depth)
    sens[...] = (obs_ray[...] - img) * img

    planes(0, 1, back_project)
    for copy in ax[0]:
        copy.start()
    planes(1, nx // 2, back_project)
    for copy in ay[0]:
        copy.start()
    own = onehot[pl.ds(pl.multiple_of(my * block, block), block), :]
    images[...] = gathered(lax.dot_general(
        pieces(img), own, (((1,), (1,)), ((), ())), preferred_element_type=F32))
    for n in range(STEPS):
        planes(0, nx, functools.partial(slopes, n, STEPS - 1 - n))
        for copy in ay[n]:
            copy.wait()
        for i in range(nx):
            PS[n, i, pl.ds(PAD - 1, 1), :] = arecv[n, 0, pl.ds(i, 1), :]
            PN[n, i, pl.ds(PAD + ny, 1), :] = arecv[n, 1, pl.ds(i, 1), :]
        planes(1, nx - 1, functools.partial(backward, n))
        for copy in ax[n]:
            copy.wait()
        edges(functools.partial(backward, n))
        if n < STEPS - 1:
            for copy in ax[n + 1] + ay[n + 1]:
                copy.start()


def per_device(gx, gy, scalar, velocity, weights, start, length, pixel, observed):
    nx, ny, nz = scalar.shape
    rays = weights.shape[0]
    vmem = pl.BlockSpec(memory_space=pltpu.VMEM)
    hbm = pl.BlockSpec(memory_space=pl.ANY)
    tall = ny + 2 * PAD
    V = pltpu.VMEM
    D = pltpu.SemaphoreType.DMA
    return pl.pallas_call(
        functools.partial(body, gx, gy),
        out_shape=(
            jax.ShapeDtypeStruct((nx, rays // gy), F32),
            jax.ShapeDtypeStruct(scalar.shape, F32),
            jax.ShapeDtypeStruct(velocity.shape, F32),
        ),
        in_specs=[hbm, hbm, hbm, vmem, vmem, vmem, vmem],
        out_specs=(vmem, vmem, vmem),
        scratch_shapes=[
            V((STEPS, nx + 2, tall, nz), F32),
            V((nx, ny, nz), F32),
            V((3, nx, ny, nz), F32),
            V((rays, nz), F32),
            V((nz, rays), F32),
            V((rays, nz), BF16),
            V((rays, nz), BF16),
            V((nx, 2 * ny, rays), BF16),
            V((rays, rays), BF16),
            V((nx, rays), F32),
            V((nx, rays), F32),
            V((STEPS, nx, ny, nz), F32),
            V((STEPS, nx + 1, ny, nz), F32),
            V((STEPS, nx + 1, ny, nz), F32),
            V((STEPS, nx, tall, nz), F32),
            V((STEPS, nx, tall, nz), F32),
            V((STEPS, 2, nx, nz), F32),
            V((STEPS, 2, nx, nz), F32),
            V((STEPS, 2, nx, nz), F32),
            V((STEPS, 2, nx, nz), F32),
            V((nx, rays), F32),
            V((gy - 1, nx, rays), F32),
            D((3,)),
            D((2 * STEPS, 2)),
            D((2 * STEPS, 2)),
            D((2 * STEPS, 2)),
            D((2 * STEPS, 2)),
            D((gy - 1,)),
            D((gy - 1,)),
        ],
        compiler_params=pltpu.CompilerParams(
            collective_id=0, has_side_effects=True, vmem_limit_bytes=60 * 2**20
        ),
    )(scalar, velocity, weights, start, length, pixel[None, :], observed)


def solution(mesh):
    in_specs = (
        P("gx", "gy", None),
        P(None, "gx", "gy", None),
        P(),
        P("gx", None),
        P("gx", None),
        P(),
        P("gx", None),
    )
    out_specs = (P("gx", "gy"), P("gx", "gy", None), P(None, "gx", "gy", None))
    return jax.shard_map(
        functools.partial(per_device, mesh.shape["gx"], mesh.shape["gy"]),
        mesh=mesh, in_specs=in_specs, out_specs=out_specs, check_vma=False,
    )
```

time: 179 us -> 55 us (0.31)
  the two profiles are of different devices: /device:TPU:28 before, /device:TPU:0 now
where the time goes in v1:
time: 55 us; the launch traced here: 54.7 us
  Pallas kernels  46.6 us (85%)
  local copies, waits for them, and re-layouts  7.45 us (14%)
  between operations  0.64 us (1%)
    pallas_call x1, Pallas kernels, per_device(): pl.pallas_call(functools.partial(body, gx, gy), out_shape=(jax.ShapeDtype...  46.6 us
    unnamed x3, local copies, waits for them, and re-layouts  7.45 us

profile of v1, /device:TPU:0, one launch (start us, length us, event | category | flops | bytes accessed | tf_op | source)
XLA Modules:
  0.0 54.7 jit_solution(17293192221419107881)
XLA Ops:
  0.6 46.6 %shard_map.94 = (f32[8,512]{1,0:T(8,128)}, f32[8,128,256]{2,1,0:T(8,128)}, f32[3,8,128,256]{3,2,1,0:T(8,128)}) custom-call(f32[8,128,256]{2,1,0:T(8,128)} %scalar.1, f32[3,8,128,256]{3,2,1,0:T(8,128)} %velocity.1, f32[1024,256]{1,0:T(8,128)} %weights.1, s32[8,1024]{1,0:T(8,128)} %start.1, s32[8,1024]{1,0:T(8,128)} %length.1, s32[1,1024]{1,0:T(1,128)} %bitcast.1, ...), custom_call_target="tpu_custom_call" | custom-call | tf_op jit(solution)/shard_map/pallas_call | solution.py:317
  47.3 1.3 %copy.13 = f32[8,512]{1,0:T(8,128)} copy(f32[8,512]{1,0:T(8,128)} %get-tuple-element.6) | data formatting | bytes 32768
  48.6 2.3 %copy.14 = f32[8,128,256]{2,1,0:T(8,128)} copy(f32[8,128,256]{2,1,0:T(8,128)} %get-tuple-element.7) | data formatting | bytes 2097152
  50.9 3.9 %copy.15 = f32[3,8,128,256]{3,2,1,0:T(8,128)} copy(f32[3,8,128,256]{3,2,1,0:T(8,128)} %get-tuple-element.8) | data formatting | bytes 6291456

commit v2 on v1

--- a/solution.py
+++ b/solution.py
@@ -10,6 +10,7 @@
 STEPS = 3
 DT = 0.1
 PAD = 8
+CUT = 32
 MESH = pl.DeviceIdType.MESH
 F32, BF16 = jnp.float32, jnp.bfloat16
 
@@ -30,7 +31,7 @@
     right, left = lax.rem(mx + 1, gx), lax.rem(mx + gx - 1, gx)
     north, south = lax.rem(my + 1, gy), lax.rem(my + gy - 1, gy)
     rows = pl.ds(PAD, ny)
-    cut = 32
+    cut = CUT
 
     local = [
         pltpu.make_async_copy(scalar, C.at[0, pl.ds(1, nx), rows], load_sem.at[0]),
@@ -48,47 +49,89 @@
         pl.semaphore_signal(barrier, inc=1, device_id=(mx, who), device_id_type=MESH)
     pl.semaphore_wait(barrier, 2 + len(peers))
 
-    def xcopies(k, to_right, at_right, to_left, at_left):
+    def xcopies(s, k, to_right, at_right, to_left, at_left):
         return [
             pltpu.make_async_remote_copy(
-                to_right, at_right, xsend.at[k, 0], xrecv.at[k, 0],
+                to_right, at_right, xsend.at[s, k, 0], xrecv.at[s, k, 0],
                 device_id=(right, my), device_id_type=MESH),
             pltpu.make_async_remote_copy(
-                to_left, at_left, xsend.at[k, 1], xrecv.at[k, 1],
+                to_left, at_left, xsend.at[s, k, 1], xrecv.at[s, k, 1],
                 device_id=(left, my), device_id_type=MESH),
         ]
 
-    def ycopies(k, stage, recv, n):
-        return [
+    def ycopies(s, stage, recv, n):
+        return [[
             pltpu.make_async_remote_copy(
-                stage.at[n, 0], recv.at[n, 0], ysend.at[k, 0], yrecv.at[k, 0],
-                device_id=(mx, north), device_id_type=MESH),
-            pltpu.make_async_remote_copy(
-                stage.at[n, 1], recv.at[n, 1], ysend.at[k, 1], yrecv.at[k, 1],
-                device_id=(mx, south), device_id_type=MESH),
-        ]
-
+                stage.at[n, g, d], recv.at[n, g, d], ysend.at[s, g, d], yrecv.at[s, g, d],
+                device_id=(mx, (north, south)[d]), device_id_type=MESH)
+            for d in range(2)] for g in range(2)]
+
+    started = []
+
+    def begin(copies):
+        for copy in copies:
+            copy.start()
+            started.append(copy)
+
+    def arrive(copies):
+        for copy in copies:
+            copy.wait_recv()
+
+    chunks = ny // cut
+    order = list(range(1, chunks - 1)) + [0, chunks - 1]
     cx, cy, ax, ay = [], [], [], []
     for n in range(STEPS):
-        cx.append(xcopies(
-            n,
-            scalar.at[nx - 1] if n == 0 else C.at[n, nx, rows], C.at[n, 0, rows],
-            scalar.at[0] if n == 0 else C.at[n, 1, rows], C.at[n, nx + 1, rows]))
+        cs, rs = [], []
+        for k in range(chunks):
+            here, at = pl.ds(k * cut, cut), pl.ds(PAD + k * cut, cut)
+            cs.append(xcopies(
+                n, k,
+                scalar.at[nx - 1, here] if n == 0 else C.at[n, nx, at], C.at[n, 0, at],
+                scalar.at[0, here] if n == 0 else C.at[n, 1, at], C.at[n, nx + 1, at]))
+            rs.append(xcopies(
+                STEPS + n, k,
+                PW.at[n, nx, here], PW.at[n, 0, here],
+                PE.at[n, 0, here], PE.at[n, nx, here]))
+        cx.append(cs)
+        ax.append(rs)
         cy.append(ycopies(n, cstage, crecv, n))
-        ax.append(xcopies(
-            STEPS + n,
-            PW.at[n, nx], PW.at[n, 0],
-            PE.at[n, 0], PE.at[n, nx]))
         ay.append(ycopies(STEPS + n, astage, arecv, n))
 
-    for copy in cx[0]:
-        copy.start()
+    for k in order:
+        begin(cx[0][k])
 
     def planes(lo, hi, f):
         lax.fori_loop(lo, hi, lambda i, x: (f(i), x)[1], 0)
 
     def edges(f):
         lax.fori_loop(0, 2, lambda t, x: (f(t * (nx - 1)), x)[1], 0)
+
+    inner, outer = range(1, nx - 1), (0, nx - 1)
+
+    def rim(n, recv, copies, low, high, ids):
+        arrive(copies)
+        g = 0 if ids is inner else 1
+        for i in ids:
+            low(i, recv[n, g, 0, pl.ds(i, 1), :])
+            high(i, recv[n, g, 1, pl.ds(i, 1), :])
+
+    def rim_c(n, ids):
+        def low(i, x):
+            C[n, i + 1, pl.ds(PAD - 1, 1), :] = x
+
+        def high(i, x):
+            C[n, i + 1, pl.ds(PAD + ny, 1), :] = x
+
+        rim(n, crecv, cy[n][0 if ids is inner else 1], low, high, ids)
+
+    def rim_a(n, ids):
+        def low(i, x):
+            PS[n, i, pl.ds(PAD - 1, 1), :] = x
+
+        def high(i, x):
+            PN[n, i, pl.ds(PAD + ny, 1), :] = x
+
+        rim(n, arecv, ay[n][0 if ids is inner else 1], low, high, ids)
 
     lane = lax.broadcasted_iota(jnp.int32, (cut, nz), 1)
 
@@ -107,12 +150,15 @@
         upper, lower = shifts_z(c, c)
         return c, east, west, up_y, down_y, upper, lower
 
-    def stage_c(n, i):
-        cstage[n, 0, pl.ds(i, 1), :] = C[n, i + 1, pl.ds(PAD + ny - 1, 1), :]
-        cstage[n, 1, pl.ds(i, 1), :] = C[n, i + 1, pl.ds(PAD, 1), :]
-
-    def forward(n, i):
-        for k in range(ny // cut):
+    def stage_c(n, ids):
+        g = 0 if ids is inner else 1
+        for i in ids:
+            cstage[n, g, 0, pl.ds(i, 1), :] = C[n, i + 1, pl.ds(PAD + ny - 1, 1), :]
+            cstage[n, g, 1, pl.ds(i, 1), :] = C[n, i + 1, pl.ds(PAD, 1), :]
+        begin(cy[n][g])
+
+    def forward(n, i, ks=range(ny // cut)):
+        for k in ks:
             c, east, west, up_y, down_y, upper, lower = around(n, i, k)
             here = pl.ds(k * cut, cut)
             u, v, w = vel[0, i, here, :], vel[1, i, here, :], vel[2, i, here, :]
@@ -123,8 +169,6 @@
                 C[n + 1, i + 1, pl.ds(PAD + k * cut, cut), :] = new
             else:
                 c3[i, here, :] = new
-        if n < STEPS - 1:
-            stage_c(n + 1, i)
 
     def make_mask(i):
         s, l = start[pl.ds(i, 1), :], length[pl.ds(i, 1), :]
@@ -185,9 +229,12 @@
         PN[n, i, pl.ds(PAD + k * cut, cut), :] = a + va
         PS[n, i, pl.ds(PAD + k * cut, cut), :] = a - va
 
-    def stage_a(n, i):
-        astage[n, 0, pl.ds(i, 1), :] = PS[n, i, pl.ds(PAD + ny - 1, 1), :]
-        astage[n, 1, pl.ds(i, 1), :] = PN[n, i, pl.ds(PAD, 1), :]
+    def stage_a(n, ids):
+        g = 0 if ids is inner else 1
+        for i in ids:
+            astage[n, g, 0, pl.ds(i, 1), :] = PS[n, i, pl.ds(PAD + ny - 1, 1), :]
+            astage[n, g, 1, pl.ds(i, 1), :] = PN[n, i, pl.ds(PAD, 1), :]
+        begin(ay[n][g])
 
     def back_project(t):
         his, los = [], []
@@ -204,10 +251,9 @@
         for j, i in enumerate((t, nx - 1 - t)):
             for k in range(ny // cut):
                 products(0, i, k, a[j * ny + k * cut:j * ny + (k + 1) * cut])
-            stage_a(0, i)
-
-    def backward(n, i):
-        for k in range(ny // cut):
+
+    def backward(n, i, ks=range(ny // cut)):
+        for k in ks:
             here = pl.ds(k * cut, cut)
             at = PAD + k * cut
             a = A[n, i, here, :]
@@ -221,8 +267,6 @@
                 products(n + 1, i, k, new)
             else:
                 grad_scalar[i, here, :] = new
-        if n < STEPS - 1:
-            stage_a(n + 1, i)
 
     def slopes(n, m, i):
         for k in range(ny // cut):
@@ -236,9 +280,8 @@
                     grad_velocity[j, i, here, :] += a * d
 
     local[0].wait()
-    planes(0, nx, functools.partial(stage_c, 0))
-    for copy in cy[0]:
-        copy.start()
+    stage_c(0, inner)
+    stage_c(0, outer)
     planes(0, nx, make_mask)
     local[1].wait()
     for n in range(STEPS):
@@ -248,20 +291,21 @@
             obs_ray[...] = gathered(g)
             local[2].wait()
             planes(0, rays // 128, split_weights)
-        for copy in cy[n]:
-            copy.wait()
-        for i in range(nx):
-            C[n, i + 1, pl.ds(PAD - 1, 1), :] = crecv[n, 0, pl.ds(i, 1), :]
-            C[n, i + 1, pl.ds(PAD + ny, 1), :] = crecv[n, 1, pl.ds(i, 1), :]
+        rim_c(n, inner)
         planes(1, nx - 1, functools.partial(forward, n))
-        if n == STEPS - 1:
+        if n < STEPS - 1:
+            stage_c(n + 1, inner)
+        else:
             planes(1, nx - 1, project)
-        for copy in cx[n]:
-            copy.wait()
-        edges(functools.partial(forward, n))
+        for k in order:
+            if k == 0:
+                rim_c(n, outer)
+            arrive(cx[n][k])
+            edges(functools.partial(forward, n, ks=(k,)))
+            if n < STEPS - 1:
+                begin(cx[n + 1][k])
         if n < STEPS - 1:
-            for copy in cx[n + 1] + cy[n + 1]:
-                copy.start()
+            stage_c(n + 1, outer)
         else:
             edges(project)
 
@@ -282,28 +326,44 @@
     sens[...] = (obs_ray[...] - img) * img
 
     planes(0, 1, back_project)
-    for copy in ax[0]:
-        copy.start()
+    for k in order:
+        begin(ax[0][k])
+    stage_a(0, outer)
     planes(1, nx // 2, back_project)
-    for copy in ay[0]:
-        copy.start()
+    stage_a(0, inner)
     own = onehot[pl.ds(pl.multiple_of(my * block, block), block), :]
     images[...] = gathered(lax.dot_general(
         pieces(img), own, (((1,), (1,)), ((), ())), preferred_element_type=F32))
     for n in range(STEPS):
         planes(0, nx, functools.partial(slopes, n, STEPS - 1 - n))
-        for copy in ay[n]:
-            copy.wait()
-        for i in range(nx):
-            PS[n, i, pl.ds(PAD - 1, 1), :] = arecv[n, 0, pl.ds(i, 1), :]
-            PN[n, i, pl.ds(PAD + ny, 1), :] = arecv[n, 1, pl.ds(i, 1), :]
+        rim_a(n, inner)
         planes(1, nx - 1, functools.partial(backward, n))
-        for copy in ax[n]:
-            copy.wait()
-        edges(functools.partial(backward, n))
         if n < STEPS - 1:
-            for copy in ax[n + 1] + ay[n + 1]:
-                copy.start()
+            stage_a(n + 1, inner)
+        for k in order:
+            if k == 0:
+                rim_a(n, outer)
+            arrive(ax[n][k])
+            edges(functools.partial(backward, n, ks=(k,)))
+            if n < STEPS - 1:
+                begin(ax[n + 1][k])
+        if n < STEPS - 1:
+            stage_a(n + 1, outer)
+    for copy in started:
+        copy.wait_send()
+
+
+def write_out(*refs):
+    count = len(refs) // 2
+    sems = refs[-1]
+    copies = [
+        pltpu.make_async_copy(a, b, sems.at[j])
+        for j, (a, b) in enumerate(zip(refs[:count], refs[count:-1]))
+    ]
+    for copy in copies:
+        copy.start()
+    for copy in copies:
+        copy.wait()
 
 
 def per_device(gx, gy, scalar, velocity, weights, start, length, pixel, observed):
@@ -314,13 +374,10 @@
     tall = ny + 2 * PAD
     V = pltpu.VMEM
     D = pltpu.SemaphoreType.DMA
-    return pl.pallas_call(
+    shapes = ((nx, rays // gy), scalar.shape, velocity.shape)
+    parts = pl.pallas_call(
         functools.partial(body, gx, gy),
-        out_shape=(
-            jax.ShapeDtypeStruct((nx, rays // gy), F32),
-            jax.ShapeDtypeStruct(scalar.shape, F32),
-            jax.ShapeDtypeStruct(velocity.shape, F32),
-        ),
+        out_shape=tuple(pltpu.VMEM(x, F32) for x in shapes),
         in_specs=[hbm, hbm, hbm, vmem, vmem, vmem, vmem],
         out_specs=(vmem, vmem, vmem),
         scratch_shapes=[
@@ -340,24 +397,32 @@
             V((STEPS, nx + 1, ny, nz), F32),
             V((STEPS, nx, tall, nz), F32),
             V((STEPS, nx, tall, nz), F32),
-            V((STEPS, 2, nx, nz), F32),
-            V((STEPS, 2, nx, nz), F32),
-            V((STEPS, 2, nx, nz), F32),
-            V((STEPS, 2, nx, nz), F32),
+            V((STEPS, 2, 2, nx, nz), F32),
+            V((STEPS, 2, 2, nx, nz), F32),
+            V((STEPS, 2, 2, nx, nz), F32),
+            V((STEPS, 2, 2, nx, nz), F32),
             V((nx, rays), F32),
             V((gy - 1, nx, rays), F32),
             D((3,)),
-            D((2 * STEPS, 2)),
-            D((2 * STEPS, 2)),
-            D((2 * STEPS, 2)),
-            D((2 * STEPS, 2)),
+            D((2 * STEPS, ny // CUT, 2)),
+            D((2 * STEPS, ny // CUT, 2)),
+            D((2 * STEPS, 2, 2)),
+            D((2 * STEPS, 2, 2)),
             D((gy - 1,)),
             D((gy - 1,)),
         ],
         compiler_params=pltpu.CompilerParams(
-            collective_id=0, has_side_effects=True, vmem_limit_bytes=60 * 2**20
+            collective_id=0, has_side_effects=True, vmem_limit_bytes=50 * 2**20
         ),
     )(scalar, velocity, weights, start, length, pixel[None, :], observed)
+    return pl.pallas_call(
+        write_out,
+        out_shape=tuple(jax.ShapeDtypeStruct(x, F32) for x in shapes),
+        in_specs=[vmem] * 3,
+        out_specs=(hbm,) * 3,
+        scratch_shapes=[D((3,))],
+        compiler_params=pltpu.CompilerParams(vmem_limit_bytes=2**20),
+    )(*parts)
 
 
 def solution(mesh):

time: 55 us -> 44.3 us (0.81)
  local copies, waits for them, and re-layouts: 7.45 us -> 0 us
  Pallas kernels: 46.6 us -> 43.4 us
    unnamed x3 -> x0, local copies, waits for them, and re-layouts: 7.45 us -> none
    pallas_call x1 -> x2, Pallas kernels: 46.6 us -> 43.4 us  [the longest x1 41.4 us: per_device(): pl.pallas_call(functools.partial(body, gx, gy), out_shape=tuple((pltpu.VM...]
where the time goes in v2:
time: 44.3 us; the launch traced here: 44.1 us
  Pallas kernels  43.4 us (98%)
  between operations  0.64 us (1%)
    pallas_call x1, Pallas kernels, per_device(): pl.pallas_call(functools.partial(body, gx, gy), out_shape=tuple((pltpu.VM...  41.4 us
    pallas_call x1, Pallas kernels, per_device(): pl.pallas_call(write_out, out_shape=tuple((jax.ShapeDtypeStruct(x, F32) f...  2.04 us

profile of v2, /device:TPU:0, one launch (start us, length us, event | category | flops | bytes accessed | tf_op | source)
XLA Modules:
  0.0 44.1 jit_solution(14016112288314193347)
XLA Ops:
  0.6 41.4 %shard_map.94 = (f32[8,512]{1,0:T(8,128)S(1)}, f32[8,128,256]{2,1,0:T(8,128)S(1)}, f32[3,8,128,256]{3,2,1,0:T(8,128)S(1)}) custom-call(f32[8,128,256]{2,1,0:T(8,128)} %scalar.1, f32[3,8,128,256]{3,2,1,0:T(8,128)} %velocity.1, f32[1024,256]{1,0:T(8,128)} %weights.1, s32[8,1024]{1,0:T(8,128)} %start.1, s32[8,1024]{1,0:T(8,128)} %length.1, s32[1,1024]{1,0:T(1,128)} %bitcast.1, ...), custom_call_target="tpu_custom_call" | custom-call | tf_op jit(solution)/shard_map/pallas_call | solution.py:378
  42.0 2.0 %shard_map.95 = (f32[8,512]{1,0:T(8,128)}, f32[8,128,256]{2,1,0:T(8,128)}, f32[3,8,128,256]{3,2,1,0:T(8,128)}) custom-call(f32[8,512]{1,0:T(8,128)S(1)} %get-tuple-element.6.refs_0_, f32[8,128,256]{2,1,0:T(8,128)S(1)} %get-tuple-element.7.refs_1_, f32[3,8,128,256]{3,2,1,0:T(8,128)S(1)} %get-tuple-element.8.refs_2_), custom_call_target="tpu_custom_call" | custom-call | tf_op jit(solution)/shard_map/pallas_call | solution.py:418

commit v3 on v2

--- a/solution.py
+++ b/solution.py
@@ -331,11 +331,13 @@
     stage_a(0, outer)
     planes(1, nx // 2, back_project)
     stage_a(0, inner)
-    own = onehot[pl.ds(pl.multiple_of(my * block, block), block), :]
-    images[...] = gathered(lax.dot_general(
-        pieces(img), own, (((1,), (1,)), ((), ())), preferred_element_type=F32))
     for n in range(STEPS):
-        planes(0, nx, functools.partial(slopes, n, STEPS - 1 - n))
+        if n == 1:
+            own = onehot[pl.ds(pl.multiple_of(my * block, block), block), :]
+            images[...] = gathered(lax.dot_general(
+                pieces(img), own, (((1,), (1,)), ((), ())), preferred_element_type=F32))
+        for m in ((), (0,), range(1, n + 1))[min(n, 2)]:
+            planes(0, nx, functools.partial(slopes, m, STEPS - 1 - m))
         rim_a(n, inner)
         planes(1, nx - 1, functools.partial(backward, n))
         if n < STEPS - 1:

time: 44.3 us -> 44.3 us (level)
  no operation moved by 1% of the time
where the time goes in v3:
time: 44.3 us; the launch traced here: 44.1 us
  Pallas kernels  43.4 us (98%)
  between operations  0.64 us (1%)
    pallas_call x1, Pallas kernels, per_device(): pl.pallas_call(functools.partial(body, gx, gy), out_shape=tuple((pltpu.VM...  41.4 us
    pallas_call x1, Pallas kernels, per_device(): pl.pallas_call(write_out, out_shape=tuple((jax.ShapeDtypeStruct(x, F32) f...  2.04 us

profile of v3, /device:TPU:0, one launch (start us, length us, event | category | flops | bytes accessed | tf_op | source)
XLA Modules:
  0.0 44.1 jit_solution(11048876578738438866)
XLA Ops:
  0.6 41.4 %shard_map.94 = (f32[8,512]{1,0:T(8,128)S(1)}, f32[8,128,256]{2,1,0:T(8,128)S(1)}, f32[3,8,128,256]{3,2,1,0:T(8,128)S(1)}) custom-call(f32[8,128,256]{2,1,0:T(8,128)} %scalar.1, f32[3,8,128,256]{3,2,1,0:T(8,128)} %velocity.1, f32[1024,256]{1,0:T(8,128)} %weights.1, s32[8,1024]{1,0:T(8,128)} %start.1, s32[8,1024]{1,0:T(8,128)} %length.1, s32[1,1024]{1,0:T(1,128)} %bitcast.1, ...), custom_call_target="tpu_custom_call" | custom-call | tf_op jit(solution)/shard_map/pallas_call | solution.py:380
  42.0 2.0 %shard_map.95 = (f32[8,512]{1,0:T(8,128)}, f32[8,128,256]{2,1,0:T(8,128)}, f32[3,8,128,256]{3,2,1,0:T(8,128)}) custom-call(f32[8,512]{1,0:T(8,128)S(1)} %get-tuple-element.6.refs_0_, f32[8,128,256]{2,1,0:T(8,128)S(1)} %get-tuple-element.7.refs_1_, f32[3,8,128,256]{3,2,1,0:T(8,128)S(1)} %get-tuple-element.8.refs_2_), custom_call_target="tpu_custom_call" | custom-call | tf_op jit(solution)/shard_map/pallas_call | solution.py:420
